TPU v7x, 32 devices: a whole 2x2x4 slice. The times are simulated.
32 devices in a mesh: ctx: 8 (over z, x), head: 4 (over y, core).
Axes of the slice: x: 2, y: 2, z: 4, core: 2. Of those that a mesh axis runs over, the one named last changes fastest.
Arguments:
- queries: bfloat16 [8192, 5120], P('ctx', 'head'), may hold values from -60 to 60
- key_rows: bfloat16 [8192, 5120], P('ctx', 'head'), may hold values from -10 to 10
- value_rows: bfloat16 [8192, 5120], P('ctx', 'head'), may hold values from -60 to 60
- norm_gain: float32 [5120], P('head'), may hold values from 0.1 to 1.9
- sort_index: int32 [32], replicated, may hold values from 0 to 31
- grad_normed: bfloat16 [8192, 5120], P('ctx', 'head'), may hold values from -6 to 6
Outputs:
- normed: bfloat16 [8192, 5120], P('ctx', 'head')
- grad_queries: bfloat16 [8192, 5120], P('ctx', 'head')
- grad_keys: bfloat16 [8192, 5120], P('ctx', 'head')
- grad_values: bfloat16 [8192, 5120], P('ctx', 'head')
Inputs may be any that keep to these rules, and one draw needn't show every extreme that they name: `sort_index`: several query blocks may name the same block.
All inputs are finite; a program needn't handle non-finite values.
Results may differ from a plain program's by a relative error of at most 0.009.
Values may be sent and summed in bfloat16 or wider, within the bound.
No kernel may reach another device: no remote copies, remote signals or barrier semaphores. Data moves between devices by JAX's collectives and lax.ppermute only.
A program may use at most 128 MiB of HBM per device.

v0:
```python
import jax
import jax.numpy as jnp
from jax import lax
from jax.sharding import PartitionSpec as P

HDIM = 128
BLOCK = 256
WIDTH = 5120


def allowed_keys(block_id):
    query_pos = jnp.arange(BLOCK)[:, None]
    key_pos = jnp.arange(BLOCK)[None, :]
    causal = key_pos <= query_pos
    before = jnp.broadcast_to(block_id > 0, (BLOCK, BLOCK))
    chosen = jnp.ones((BLOCK, BLOCK), dtype=jnp.bool_)
    return jnp.concatenate([causal, before, chosen], axis=1)


def probabilities(query_block, key_set, allowed):
    head_count = query_block.shape[1] // HDIM
    q_split = query_block.reshape(BLOCK, head_count, HDIM)
    k_split = key_set.reshape(3 * BLOCK, head_count, HDIM)
    scores = jnp.einsum(
        "qhd,khd->hqk", q_split, k_split, preferred_element_type=jnp.float32
    ) * HDIM ** (-0.5)
    scores = jnp.where(allowed[None], scores, -jnp.inf)
    highest = jnp.max(scores, axis=2, keepdims=True)
    weights = jnp.exp(scores - highest)
    return weights / jnp.sum(weights, axis=2, keepdims=True)


def block_forward(items):
    query_block, key_set, value_set, block_id = items
    head_count = query_block.shape[1] // HDIM
    probs = probabilities(query_block, key_set, allowed_keys(block_id))
    probs_low = probs.astype(jnp.bfloat16)
    v_split = value_set.reshape(3 * BLOCK, head_count, HDIM)
    result = jnp.einsum("hqk,khd->qhd", probs_low, v_split, preferred_element_type=jnp.float32)
    return result.reshape(BLOCK, head_count * HDIM)


def block_backward(items):
    query_block, key_set, value_set, block_id, grad_block = items
    head_count = query_block.shape[1] // HDIM
    feature_cols = head_count * HDIM
    probs = probabilities(query_block, key_set, allowed_keys(block_id))
    probs_low = probs.astype(jnp.bfloat16)
    q_split = query_block.reshape(BLOCK, head_count, HDIM)
    k_split = key_set.reshape(3 * BLOCK, head_count, HDIM)
    v_split = value_set.reshape(3 * BLOCK, head_count, HDIM)
    d_split = grad_block.reshape(BLOCK, head_count, HDIM)
    grad_set_v = jnp.einsum(
        "hqk,qhd->khd", probs_low, d_split, preferred_element_type=jnp.float32
    ).reshape(3 * BLOCK, feature_cols)
    grad_probs = jnp.einsum("qhd,khd->hqk", d_split, v_split, preferred_element_type=jnp.float32)
    row_center = jnp.sum(probs * grad_probs, axis=2, keepdims=True)
    grad_scores = (probs * (grad_probs - row_center) * HDIM ** (-0.5)).astype(jnp.bfloat16)
    grad_q = jnp.einsum("hqk,khd->qhd", grad_scores, k_split, preferred_element_type=jnp.float32)
    grad_q = grad_q.reshape(BLOCK, feature_cols).astype(jnp.bfloat16)
    grad_set_k = jnp.einsum(
        "hqk,qhd->khd", grad_scores, q_split, preferred_element_type=jnp.float32
    ).reshape(3 * BLOCK, feature_cols)
    return (
        grad_q,
        grad_set_k[:BLOCK],
        grad_set_k[BLOCK:].astype(jnp.bfloat16),
        grad_set_v[:BLOCK],
        grad_set_v[BLOCK:].astype(jnp.bfloat16),
    )


def to_slices(key_rows, value_rows, ctx_size):
    blocks = key_rows.shape[0] // BLOCK
    shaped = (blocks, ctx_size, BLOCK // ctx_size, key_rows.shape[1])
    return (
        lax.all_to_all(key_rows.reshape(shaped), "ctx", split_axis=1, concat_axis=0, tiled=True),
        lax.all_to_all(value_rows.reshape(shaped), "ctx", split_axis=1, concat_axis=0, tiled=True),
    )


def from_slices(sliced, picks, ctx_size):
    groups = picks.shape[1]
    blocks = picks.shape[0] // ctx_size
    flat = picks.reshape(-1)

    def select(member):
        chosen = jnp.take(member, flat, axis=0)
        return chosen.reshape(ctx_size, blocks * groups, 1, member.shape[2], member.shape[3])

    arrived = (
        lax.all_to_all(select(sliced[0]), "ctx", split_axis=0, concat_axis=2, tiled=True),
        lax.all_to_all(select(sliced[1]), "ctx", split_axis=0, concat_axis=2, tiled=True),
    )

    def finish(member):
        return member.reshape(blocks, groups, ctx_size * member.shape[3], member.shape[4])

    return (finish(arrived[0]), finish(arrived[1]))


def grads_home(terms, picks, valid, ctx_size):
    blocks, groups = (terms[0].shape[0], terms[0].shape[1])
    feature_cols = terms[0].shape[3]
    slice_rows = BLOCK // ctx_size
    block_count = blocks * ctx_size
    shaped = (blocks * groups, ctx_size, slice_rows, feature_cols)
    sliced = (
        lax.all_to_all(terms[0].reshape(shaped), "ctx", split_axis=1, concat_axis=0, tiled=True),
        lax.all_to_all(terms[1].reshape(shaped), "ctx", split_axis=1, concat_axis=0, tiled=True),
    )
    targets = jnp.arange(block_count, dtype=jnp.int32)[:, None]
    table = ((picks.reshape(-1)[None, :] == targets) & valid.reshape(-1)[None, :]).astype(
        jnp.bfloat16
    )

    def gather_sum(member):
        summed = jnp.dot(
            table, member.reshape(member.shape[0], -1), preferred_element_type=jnp.float32
        )
        return summed.reshape(ctx_size, blocks, 1, slice_rows, feature_cols)

    arrived = (
        lax.all_to_all(
            gather_sum(sliced[0]).astype(jnp.bfloat16),
            "ctx",
            split_axis=0,
            concat_axis=2,
            tiled=True,
        ).astype(jnp.float32),
        lax.all_to_all(
            gather_sum(sliced[1]).astype(jnp.bfloat16),
            "ctx",
            split_axis=0,
            concat_axis=2,
            tiled=True,
        ).astype(jnp.float32),
    )
    return (
        arrived[0].reshape(blocks, BLOCK, feature_cols),
        arrived[1].reshape(blocks, BLOCK, feature_cols),
    )


def on_device(queries, key_rows, value_rows, norm_gain, sort_index, grad_normed):
    ctx_size = lax.axis_size("ctx")
    feature_cols = queries.shape[1]
    blocks = queries.shape[0] // BLOCK
    block_count = blocks * ctx_size
    first_block = lax.axis_index("ctx") * blocks
    block_ids = first_block + jnp.arange(blocks, dtype=jnp.int32)
    all_ids = jnp.arange(block_count, dtype=jnp.int32)
    before_ids = jnp.maximum(all_ids - 1, 0)
    own_keys = key_rows.reshape(blocks, BLOCK, feature_cols)
    own_values = value_rows.reshape(blocks, BLOCK, feature_cols)
    q_blocks = queries.reshape(blocks, BLOCK, feature_cols)
    sliced = to_slices(key_rows, value_rows, ctx_size)
    picks = jnp.stack([before_ids, sort_index], axis=1)
    far_keys, far_values = from_slices(sliced, picks, ctx_size)
    before_keys = far_keys[:, 0]
    before_values = far_values[:, 0]
    sorted_keys = far_keys[:, 1]
    sorted_values = far_values[:, 1]
    key_sets = jnp.concatenate([own_keys, before_keys, sorted_keys], axis=1)
    value_sets = jnp.concatenate([own_values, before_values, sorted_values], axis=1)
    key_sets, value_sets = (key_sets, value_sets)
    attended = lax.map(block_forward, (q_blocks, key_sets, value_sets, block_ids))
    attended = attended.reshape(blocks * BLOCK, feature_cols)
    lifted = norm_gain * grad_normed.astype(jnp.float32)
    squares, center = lax.psum(
        (jnp.sum(attended * attended, axis=1), jnp.sum(lifted * attended, axis=1)), "head"
    )
    inv_rms = lax.rsqrt(squares[:, None] / WIDTH + 1e-05)
    normed = (attended * inv_rms * norm_gain).astype(jnp.bfloat16)
    grad_attended = (inv_rms * lifted - attended * inv_rms**3 * center[:, None] / WIDTH).astype(
        jnp.bfloat16
    )
    g_blocks = grad_attended.reshape(blocks, BLOCK, feature_cols)
    grad_q, own_k, far_k, own_v, far_v = lax.map(
        block_backward, (q_blocks, key_sets, value_sets, block_ids, g_blocks)
    )
    picks = jnp.stack([before_ids, sort_index], axis=1)
    valid = jnp.stack([all_ids > 0, all_ids >= 0], axis=1)
    routed_k, routed_v = grads_home(
        (
            far_k.reshape(blocks, 2, BLOCK, feature_cols),
            far_v.reshape(blocks, 2, BLOCK, feature_cols),
        ),
        picks,
        valid,
        ctx_size,
    )
    total_k = own_k + routed_k
    total_v = own_v + routed_v
    grad_keys = total_k.astype(jnp.bfloat16).reshape(blocks * BLOCK, feature_cols)
    grad_values = total_v.astype(jnp.bfloat16).reshape(blocks * BLOCK, feature_cols)
    return (normed, grad_q.reshape(blocks * BLOCK, feature_cols), grad_keys, grad_values)


def solution(mesh):
    in_specs = (
        P("ctx", "head"),
        P("ctx", "head"),
        P("ctx", "head"),
        P("head"),
        P(),
        P("ctx", "head"),
    )
    out_specs = (P("ctx", "head"), P("ctx", "head"), P("ctx", "head"), P("ctx", "head"))
    return jax.shard_map(
        on_device, mesh=mesh, in_specs=in_specs, out_specs=out_specs, check_vma=False
    )
```

profile of v0, /device:TPU:0, one launch (start us, length us, event | category | flops | bytes accessed | tf_op | source)
XLA Modules:
  0.0 1259.6 jit_solution(9632923343970081791)
XLA Ops:
  14.8 56.0 %all-to-all-done = bf16[4,8,32,1280]{3,2,0,1:T(8,128)(2,1)S(1)} async-done(((bf16[4,8,32,1280]{3,2,0,1:T(8,128)(2,1)}), bf16[4,8,32,1280]{3,2,0,1:T(8,128)(2,1)S(1)}, u32[]{:S(2)}, u32[]{:S(2)}) %all-to-all-start) | async-done | bytes 2621472 | tf_op jit(solution)/shard_map/all_to_all | solution.py:78
  78.8 55.4 %all-to-all-done.2 = bf16[4,8,32,1280]{3,2,0,1:T(8,128)(2,1)} async-done(((bf16[4,8,32,1280]{3,2,0,1:T(8,128)(2,1)}), bf16[4,8,32,1280]{3,2,0,1:T(8,128)(2,1)}, u32[]{:S(2)}, u32[]{:S(2)}) %all-to-all-start.2) | async-done | bytes 2621472 | tf_op jit(solution)/shard_map/all_to_all | solution.py:77
  139.2 8.9 bitcast_select_fusion
  148.1 119.8 %all_to_all.114 = bf16[8,8,1,32,1280]{4,3,1,2,0:T(8,128)(2,1)} all-to-all(bf16[8,8,1,32,1280]{4,3,1,2,0:T(8,128)(2,1)} %bitcast.264), channel_id=1, replica_groups=mesh['ctx'=8,'head'=4] {'ctx'}, dimensions={0} | all-to-all | bytes 10485760 | tf_op jit(solution)/shard_map/all_to_all | solution.py:93
  280.3 107.1 %all-to-all-done.3 = bf16[8,8,1,32,1280]{4,3,1,2,0:T(8,128)(2,1)} async-done(((bf16[8,8,1,32,1280]{4,3,1,2,0:T(8,128)(2,1)}), bf16[8,8,1,32,1280]{4,3,1,2,0:T(8,128)(2,1)}, u32[]{:S(2)}, u32[]{:S(2)}) %all-to-all-start.3) | async-done | bytes 5242912 | tf_op jit(solution)/shard_map/all_to_all | solution.py:92
  395.7 10.6 copy.99
  412.3 10.6 copy.97
  422.9 76.9 %while.28 = (s32[]{:T(128)}, f32[4,256,1280]{1,2,0:T(8,128)}, bf16[4,768,1280]{1,2,0:T(8,128)(2,1)}, s32[4]{0:T(128)S(1)}, bf16[4,256,1280]{1,2,0:T(8,128)(2,1)}...) while((s32[]{:T(128)}, f32[4,256,1280]{1,2,0:T(8,128)}, ...), condition=%wide.region_3.5_spmd, body=%wide.region_0.4_spmd.sunk | while | flops 1018888960 | bytes 33972368 | solution.py:167
  467.6 7.6 fusion.107
  523.0 356.7 %while.29 = (s32[]{:T(128)}, bf16[4,256,1280]{2,1,0:T(8,128)(2,1)}, f32[4,256,1280]{2,1,0:T(8,128)}, bf16[4,512,1280]{2,1,0:T(8,128)(2,1)}, f32[4,256,1280]{2,1,...) while((s32[]{:T(128)}, bf16[4,256,1280]{2,1,0:T(8,128)(2,1)}, ...), condition=%wide.region_12.14_spmd, body=%wide.region_8.13_spmd.sunk | while | flops 2556697856 | bytes 134263120 | solution.py:179
  540.1 24.5 %fusion.121 = bf16[10,128,256]{2,1,0:T(8,128)(2,1)} fusion(bf16[768,10,128]{0,2,1:T(8,128)(2,1)S(1)} %bitcast.254, f32[10,256,768]{2,1,0:T(8,128)} %fusion.119, f32[10,256,768]{2,1,0:T(8,128)} %get-tuple-element.335, f32[10,256]{1,0:T(8,128)S(1)} %get-tuple-element.336), kind=kOutput, calls=%fused_computation.40.clone.1 | convolution fusion | flops 517410048 | bytes 18360320 | tf_op jit(solution)/shard_map/while/body/eval_jaxpr/hqk,khd->qhd/dot_general | solution.py:59
  564.5 25.5 %fusion.123 = f32[768,10,128]{0,2,1:T(8,128)} fusion(bf16[256,10,128]{0,2,1:T(8,128)(2,1)S(1)} %bitcast.266, f32[10,256,768]{2,1,0:T(8,128)} %fusion.119, f32[10,256,768]{2,1,0:T(8,128)} %get-tuple-element.335, f32[10,256]{1,0:T(8,128)S(1)} %get-tuple-element.336), kind=kOutput, calls=%fused_computation.38.clone.1 | convolution fusion | flops 517082368 | bytes 20326400 | tf_op jit(solution)/shard_map/while/body/eval_jaxpr/hqk,qhd->khd/dot_general | solution.py:61
  629.2 24.5 %fusion.121 = bf16[10,128,256]{2,1,0:T(8,128)(2,1)} fusion(bf16[768,10,128]{0,2,1:T(8,128)(2,1)S(1)} %bitcast.254, f32[10,256,768]{2,1,0:T(8,128)} %fusion.119, f32[10,256,768]{2,1,0:T(8,128)} %get-tuple-element.335, f32[10,256]{1,0:T(8,128)S(1)} %get-tuple-element.336), kind=kOutput, calls=%fused_computation.40.clone.1 | convolution fusion | flops 517410048 | bytes 18360320 | tf_op jit(solution)/shard_map/while/body/eval_jaxpr/hqk,khd->qhd/dot_general | solution.py:59
  653.7 25.5 %fusion.123 = f32[768,10,128]{0,2,1:T(8,128)} fusion(bf16[256,10,128]{0,2,1:T(8,128)(2,1)S(1)} %bitcast.266, f32[10,256,768]{2,1,0:T(8,128)} %fusion.119, f32[10,256,768]{2,1,0:T(8,128)} %get-tuple-element.335, f32[10,256]{1,0:T(8,128)S(1)} %get-tuple-element.336), kind=kOutput, calls=%fused_computation.38.clone.1 | convolution fusion | flops 517082368 | bytes 20326400 | tf_op jit(solution)/shard_map/while/body/eval_jaxpr/hqk,qhd->khd/dot_general | solution.py:61
  718.4 24.5 %fusion.121 = bf16[10,128,256]{2,1,0:T(8,128)(2,1)} fusion(bf16[768,10,128]{0,2,1:T(8,128)(2,1)S(1)} %bitcast.254, f32[10,256,768]{2,1,0:T(8,128)} %fusion.119, f32[10,256,768]{2,1,0:T(8,128)} %get-tuple-element.335, f32[10,256]{1,0:T(8,128)S(1)} %get-tuple-element.336), kind=kOutput, calls=%fused_computation.40.clone.1 | convolution fusion | flops 517410048 | bytes 18360320 | tf_op jit(solution)/shard_map/while/body/eval_jaxpr/hqk,khd->qhd/dot_general | solution.py:59
  742.9 25.5 %fusion.123 = f32[768,10,128]{0,2,1:T(8,128)} fusion(bf16[256,10,128]{0,2,1:T(8,128)(2,1)S(1)} %bitcast.266, f32[10,256,768]{2,1,0:T(8,128)} %fusion.119, f32[10,256,768]{2,1,0:T(8,128)} %get-tuple-element.335, f32[10,256]{1,0:T(8,128)S(1)} %get-tuple-element.336), kind=kOutput, calls=%fused_computation.38.clone.1 | convolution fusion | flops 517082368 | bytes 20326400 | tf_op jit(solution)/shard_map/while/body/eval_jaxpr/hqk,qhd->khd/dot_general | solution.py:61
  807.5 24.5 %fusion.121 = bf16[10,128,256]{2,1,0:T(8,128)(2,1)} fusion(bf16[768,10,128]{0,2,1:T(8,128)(2,1)S(1)} %bitcast.254, f32[10,256,768]{2,1,0:T(8,128)} %fusion.119, f32[10,256,768]{2,1,0:T(8,128)} %get-tuple-element.335, f32[10,256]{1,0:T(8,128)S(1)} %get-tuple-element.336), kind=kOutput, calls=%fused_computation.40.clone.1 | convolution fusion | flops 517410048 | bytes 18360320 | tf_op jit(solution)/shard_map/while/body/eval_jaxpr/hqk,khd->qhd/dot_general | solution.py:59
  832.0 25.5 %fusion.123 = f32[768,10,128]{0,2,1:T(8,128)} fusion(bf16[256,10,128]{0,2,1:T(8,128)(2,1)S(1)} %bitcast.266, f32[10,256,768]{2,1,0:T(8,128)} %fusion.119, f32[10,256,768]{2,1,0:T(8,128)} %get-tuple-element.335, f32[10,256]{1,0:T(8,128)S(1)} %get-tuple-element.336), kind=kOutput, calls=%fused_computation.38.clone.1 | convolution fusion | flops 517082368 | bytes 20326400 | tf_op jit(solution)/shard_map/while/body/eval_jaxpr/hqk,qhd->khd/dot_general | solution.py:61
  895.4 110.3 %all-to-all-done.6 = bf16[8,8,32,1280]{3,2,0,1:T(8,128)(2,1)} async-done(((bf16[8,8,32,1280]{3,2,0,1:T(8,128)(2,1)}), bf16[8,8,32,1280]{3,2,0,1:T(8,128)(2,1)}, u32[]{:S(2)}, u32[]{:S(2)}) %all-to-all-start.6) | async-done | bytes 5242912 | tf_op jit(solution)/shard_map/all_to_all | solution.py:110
  1010.7 8.7 fusion.57
  1021.5 103.9 %all-to-all-done.4 = bf16[8,8,32,1280]{3,2,0,1:T(8,128)(2,1)} async-done(((bf16[8,8,32,1280]{3,2,0,1:T(8,128)(2,1)}), bf16[8,8,32,1280]{3,2,0,1:T(8,128)(2,1)}, u32[]{:S(2)}, u32[]{:S(2)}) %all-to-all-start.4) | async-done | bytes 5242912 | tf_op jit(solution)/shard_map/all_to_all | solution.py:109
  1129.3 8.7 fusion.58
  1140.0 48.8 %all-to-all-done.7 = bf16[8,4,1,32,1280]{4,3,1,2,0:T(8,128)(2,1)S(1)} async-done(((bf16[8,4,1,32,1280]{4,3,1,2,0:T(8,128)(2,1)}), bf16[8,4,1,32,1280]{4,3,1,2,0:T(8,128)(2,1)S(1)}, u32[]{:S(2)}, u32[]{:S(2)}) %all-to-all-start.7) | async-done | bytes 2621472 | tf_op jit(solution)/shard_map/all_to_all | solution.py:131
  1198.4 53.9 %all-to-all-done.5 = bf16[8,4,1,32,1280]{4,3,1,2,0:T(8,128)(2,1)} async-done(((bf16[8,4,1,32,1280]{4,3,1,2,0:T(8,128)(2,1)}), bf16[8,4,1,32,1280]{4,3,1,2,0:T(8,128)(2,1)}, u32[]{:S(2)}, u32[]{:S(2)}) %all-to-all-start.5) | async-done | bytes 2621472 | tf_op jit(solution)/shard_map/all_to_all | solution.py:124
  (253 shorter events, 341.9 us)
Async XLA Ops:
  4.1 66.7 %all-to-all-start = ((bf16[4,8,32,1280]{3,2,0,1:T(8,128)(2,1)}), bf16[4,8,32,1280]{3,2,0,1:T(8,128)(2,1)S(1)}, u32[]{:S(2)}, u32[]{:S(2)}) async-start(bf16[4,8,32,1280]{3,2,0,1:T(8,128)(2,1)} %copy.89), calls=%async_computation | async-start | bytes 5242880 | tf_op jit(solution)/shard_map/all_to_all | solution.py:78
  11.3 63.9 %copy-start.9 = (s32[32]{0:T(128)S(1)}, s32[32]{0:T(128)}, u32[]{:S(2)}) copy-start(s32[32]{0:T(128)} %param.16) | copy-start | bytes 388
  70.8 63.4 %all-to-all-start.2 = ((bf16[4,8,32,1280]{3,2,0,1:T(8,128)(2,1)}), bf16[4,8,32,1280]{3,2,0,1:T(8,128)(2,1)}, u32[]{:S(2)}, u32[]{:S(2)}) async-start(bf16[4,8,32,1280]{3,2,0,1:T(8,128)(2,1)} %copy.93), calls=%async_computation.2 | async-start | bytes 5242880 | tf_op jit(solution)/shard_map/all_to_all | solution.py:77
  267.9 5.0 copy-start.5
  267.9 119.5 %all-to-all-start.3 = ((bf16[8,8,1,32,1280]{4,3,1,2,0:T(8,128)(2,1)}), bf16[8,8,1,32,1280]{4,3,1,2,0:T(8,128)(2,1)}, u32[]{:S(2)}, u32[]{:S(2)}) async-start(bf16[8,8,1,32,1280]{4,3,1,2,0:T(8,128)(2,1)} %bitcast.263), calls=%async_computation.3 | async-start | bytes 10485760 | tf_op jit(solution)/shard_map/all_to_all | solution.py:92
  502.7 6.1 copy-start.3
  502.7 6.1 copy-start.6
  590.0 6.2 copy-start.2
  604.9 5.7 copy-start
  606.3 4.3 copy-start.1
  679.1 6.2 copy-start.2
  694.1 5.7 copy-start
  695.5 4.3 copy-start.1
  768.4 6.2 copy-start.2
  783.3 5.7 copy-start
  784.7 4.2 copy-start.1
  857.5 6.2 copy-start.2
  872.4 5.7 copy-start
  873.8 4.3 copy-start.1
  885.0 120.8 %all-to-all-start.6 = ((bf16[8,8,32,1280]{3,2,0,1:T(8,128)(2,1)}), bf16[8,8,32,1280]{3,2,0,1:T(8,128)(2,1)}, u32[]{:S(2)}, u32[]{:S(2)}) async-start(bf16[8,8,32,1280]{3,2,0,1:T(8,128)(2,1)} %copy.114), calls=%async_computation.6 | async-start | bytes 10485760 | tf_op jit(solution)/shard_map/all_to_all | solution.py:110
  895.4 115.3 %copy-start.8 = (s32[64]{0:T(128)S(1)}, s32[64]{0:T(128)}, u32[]{:S(2)}) copy-start(s32[64]{0:T(128)} %copy-done.7) | copy-start | bytes 772
  1005.8 119.6 %all-to-all-start.4 = ((bf16[8,8,32,1280]{3,2,0,1:T(8,128)(2,1)}), bf16[8,8,32,1280]{3,2,0,1:T(8,128)(2,1)}, u32[]{:S(2)}, u32[]{:S(2)}) async-start(bf16[8,8,32,1280]{3,2,0,1:T(8,128)(2,1)} %copy.108), calls=%async_computation.4 | async-start | bytes 10485760 | tf_op jit(solution)/shard_map/all_to_all | solution.py:109
  1125.3 63.5 %all-to-all-start.7 = ((bf16[8,4,1,32,1280]{4,3,1,2,0:T(8,128)(2,1)}), bf16[8,4,1,32,1280]{4,3,1,2,0:T(8,128)(2,1)S(1)}, u32[]{:S(2)}, u32[]{:S(2)}) async-start(bf16[8,4,1,32,1280]{4,3,1,2,0:T(8,128)(2,1)} %copy.116), calls=%async_computation.7 | async-start | bytes 5242880 | tf_op jit(solution)/shard_map/all_to_all | solution.py:131
  1188.9 63.4 %all-to-all-start.5 = ((bf16[8,4,1,32,1280]{4,3,1,2,0:T(8,128)(2,1)}), bf16[8,4,1,32,1280]{4,3,1,2,0:T(8,128)(2,1)}, u32[]{:S(2)}, u32[]{:S(2)}) async-start(bf16[8,4,1,32,1280]{4,3,1,2,0:T(8,128)(2,1)} %copy.110), calls=%async_computation.5 | async-start | bytes 5242880 | tf_op jit(solution)/shard_map/all_to_all | solution.py:124
  (10 other events, 27.8 us)
where the time goes:
time: 1270 us; the launch traced here: 1260 us
  waiting for transfers between devices  536 us (42%)
  matrix products  327 us (26%)
  local copies, waits for them, and re-layouts  186 us (15%)
  blocking collectives  126 us (10%)
  other arithmetic  42.7 us (3%)
  starting transfers between devices  34.7 us (3%)
    all_to_all x1, blocking collectives, from_slices(): lax.all_to_all(select(sliced[1]), 'ctx', split_axis=0, concat_axis=2, til...  120 us
    all_to_all x1, waiting for transfers between devices, grads_home(): lax.all_to_all(terms[1].reshape(shaped), 'ctx', split_axis=1, concat_axis...  110 us
    all_to_all x1, waiting for transfers between devices, from_slices(): lax.all_to_all(select(sliced[0]), 'ctx', split_axis=0, concat_axis=2, til...  107 us
    all_to_all x1, waiting for transfers between devices, grads_home(): lax.all_to_all(terms[0].reshape(shaped), 'ctx', split_axis=1, concat_axis...  104 us
    dot_general x4, matrix products, block_backward(): jnp.einsum('hqk,qhd->khd', grad_scores, q_split, preferred_element_type=j...  102 us
    dot_general x4, matrix products, block_backward(): jnp.einsum('hqk,khd->qhd', grad_scores, k_split, preferred_element_type=j...  97.9 us
    all_to_all x1, waiting for transfers between devices, to_slices(): lax.all_to_all(value_rows.reshape(shaped), 'ctx', split_axis=1, concat_ax...  56 us
    all_to_all x1, waiting for transfers between devices, to_slices(): lax.all_to_all(key_rows.reshape(shaped), 'ctx', split_axis=1, concat_axis...  55.4 us
  transfers between devices with their start and end apart: 7, of which 7 were waited for; matrix products, arithmetic and copies ran while one was open for 4% of the time, Pallas kernels for 0%

commit v1 on v0

v1 whole, which is shorter than its diff:
```python
import functools
import math

import jax
import jax.numpy as jnp
import numpy as np
from jax import lax
from jax.experimental import pallas as pl
from jax.experimental.pallas import tpu as pltpu
from jax.sharding import PartitionSpec as P

HDIM = 128
BLOCK = 256
WIDTH = 5120
LANES = 128
ROW = 16
LEAD = 2
FIRST = 1024
STATIC_SLOTS = 9
SCALE = HDIM ** (-0.5)
SCALE_LOG2 = SCALE * math.log2(math.e)
ANY = pl.BlockSpec(memory_space=pl.ANY)
SMEM = pl.BlockSpec(memory_space=pltpu.SMEM)
VMEM = pl.BlockSpec(memory_space=pltpu.VMEM)
BIG = pltpu.CompilerParams(vmem_limit_bytes=56 * 1024 * 1024)


class Layout:
    def __init__(self, ctx_size, blocks):
        self.ctx_size = ctx_size
        self.blocks = blocks
        self.levels = ctx_size // 2
        line = self.levels * blocks
        self.value_line = line
        self.value_own = 2 * line
        self.over = 2 * line + blocks
        self.places = self.over + 2 * (blocks + 1)
        self.slots = 2 * (2 * line + 2 * self.levels + 2 * blocks + 4)
        self.rows = self.slots + 2 * LEAD
        self.info = self.rows * ROW
        self.key_picks = self.info
        self.value_picks = self.info + blocks + 1
        self.total = self.info + 2 * blocks + 2
        self.device = self.info + 2 * blocks + 3


def shift_rows(array, count, rows):
    n = array.shape[0]
    if abs(count) >= n:
        return jnp.zeros_like(array)
    rolled = pltpu.roll(array, (-count) % n, 0)
    inside = (rows < n - count) if count > 0 else (rows >= -count)
    return jnp.where(inside, rolled, 0.0)


def table_kernel(picks_ref, owner_ref, block_ref, kind_ref, place_ref, out_ref, *, lay):
    n = lay.ctx_size
    blocks = lay.blocks
    width = owner_ref.shape[1]
    rows = lax.broadcasted_iota(jnp.int32, (n, width), 0)
    lanes = lax.broadcasted_iota(jnp.int32, (n, width), 1)
    out_lanes = lax.broadcasted_iota(jnp.int32, (n, LANES), 1)
    owner = owner_ref[...]
    block = block_ref[...]
    values = kind_ref[...] == 1
    place = place_ref[...]
    picks = picks_ref[...]
    side = rows & 1
    level = rows >> 1
    same_side = side == (owner & 1)
    travels = jnp.logical_xor(same_side, values)
    owned = owner == rows

    def other(array):
        return jnp.where(side == 0, pltpu.roll(array, n - 1, 0), pltpu.roll(array, 1, 0))

    need = jnp.zeros((n, width), jnp.float32)
    for j in range(blocks + 1):
        need = jnp.where(picks[:, j : j + 1] == block, 1.0, need)
    need = jnp.where(owned, 0.0, need)
    across = other(need)
    wanted = jnp.maximum(need, across)
    final = jnp.where(travels, across, 0.0)
    hops = jnp.where(wanted > 0, 1.0 + final, 0.0)
    up_hops = jnp.zeros_like(need)
    down_hops = jnp.zeros_like(need)
    for k in range(1, lay.levels):
        above = shift_rows(hops, 2 * k, rows)
        below = shift_rows(hops, -2 * k, rows)
        up_hops = jnp.maximum(up_hops, jnp.where(above > 0, above + (k - 1), 0.0))
        down_hops = jnp.maximum(down_hops, jnp.where(below > 0, below + (k - 1), 0.0))
    up = jnp.where(travels & (level >= (owner >> 1)) & (up_hops > 0), 1.0, 0.0)
    down = jnp.where(travels & (level <= (owner >> 1)) & (down_hops > 0), 1.0, 0.0)
    source = owned & jnp.logical_not(travels)
    most = jnp.maximum(up_hops, down_hops)
    over = jnp.where(source & ((most > 0) | (across > 0)), 1.0, final)
    spread = jnp.minimum(jnp.sum(need, axis=0, keepdims=True), 3.0)
    low = (width - 1 - lanes).astype(jnp.float32)
    up_rank = (up_hops * 4.0 + spread) * width + low
    down_rank = (down_hops * 4.0 + spread) * width + low
    over_rank = jnp.where(source, most * 4.0 + spread, 2.0) * width + low
    first_over = float(lay.over)

    out_ref[...] = jnp.full(out_ref.shape, -1, jnp.int32)

    def pick(pending, have, rank):
        score = jnp.where(pending * have > 0, rank, -1.0)
        best = jnp.max(score, axis=1, keepdims=True)
        return jnp.where((score == best) & (best >= 0), 1.0, 0.0)

    def where(chosen):
        return jnp.sum(chosen * (place + 1.0), axis=1, keepdims=True) - 1.0

    def pending(state):
        t, have, fresh, up, down, over, over_place, count = state
        return (t < lay.slots) & (jnp.sum(up + down + over) > 0)

    def step(state):
        t, have, fresh, up, down, over, over_place, count = state
        send_up = pick(up, have, up_rank)
        send_down = pick(down, have, down_rank)
        send_over = pick(over, have, over_rank)
        up = up - send_up
        down = down - send_down
        over = over - send_over
        got_up = shift_rows(send_up, -2, rows)
        got_down = shift_rows(send_down, 2, rows)
        got_over = other(send_over)
        got_final = jnp.where(travels, 0.0, got_over)
        any_final = jnp.max(got_final, axis=1, keepdims=True)
        over_at = jnp.where(any_final > 0, count + first_over, where(got_over))
        last = jnp.where((up + down + over + need > 0) | owned, 0.0, float(FIRST))

        def first_back(chosen):
            return jnp.max(chosen * last, axis=1, keepdims=True)

        columns = (
            where(send_up) + first_back(send_up),
            where(send_down) + first_back(send_down * (1.0 - send_up)),
            where(send_over) + first_back(send_over * (1.0 - send_up) * (1.0 - send_down)),
            where(got_up),
            where(got_down),
            over_at,
        )
        row = jnp.full((n, LANES), -1.0, jnp.float32)
        for k, column in enumerate(columns):
            row = jnp.where(out_lanes == k, column, row)
        out_ref[t + LEAD] = row.astype(jnp.int32)
        over_place = jnp.where(got_final > 0, count + first_over, over_place)
        have = jnp.maximum(have, fresh)
        fresh = jnp.maximum(got_up, jnp.maximum(got_down, got_over))
        return (t + 1, have, fresh, up, down, over, over_place, count + any_final)

    zeros = jnp.zeros_like(need)
    have = jnp.where(owned, 1.0, 0.0)
    state = (jnp.int32(0), have, zeros, up, down, over, zeros, jnp.zeros((n, 1), jnp.float32))
    state = lax.while_loop(pending, step, state)
    at = jnp.where(travels | owned, place, state[6])
    own_row = lax.broadcasted_iota(jnp.int32, (n, LANES), 0)
    row = jnp.zeros((n, LANES), jnp.float32)
    for kind in range(2):
        base = (own_row >> 1) * blocks if kind == 0 else jnp.full((n, LANES), lay.value_own)
        for j in range(blocks + 1):
            chosen = (picks[:, j : j + 1] == block) & (values if kind else jnp.logical_not(values))
            found = jnp.sum(jnp.where(chosen, at, 0.0), axis=1, keepdims=True)
            found = jnp.where(picks[:, j : j + 1] < 0, base[:, :1].astype(jnp.float32), found)
            row = jnp.where(out_lanes == kind * (blocks + 1) + j, found, row)
    row = jnp.where(out_lanes == 2 * blocks + 2, state[0].astype(jnp.float32), row)
    row = jnp.where(out_lanes == 2 * blocks + 3, own_row.astype(jnp.float32), row)
    out_ref[lay.rows] = row.astype(jnp.int32)


def routing_table(sort_index, lay):
    n, blocks = lay.ctx_size, lay.blocks
    count = n * blocks
    width = -(-2 * count // LANES) * LANES
    block = np.full(width, -2, np.int32)
    kind = np.zeros(width, np.int32)
    block[:count] = np.arange(count)
    block[count : 2 * count] = np.arange(count)
    kind[count : 2 * count] = 1
    owner = np.where(block >= 0, block // blocks, -2).astype(np.int32)
    device = np.arange(n)[:, None]
    line = np.where(block >= 0, (block // (2 * blocks)) * blocks + block % blocks, 0)[None]
    place = np.where(kind[None] == 1, lay.value_line + line, line)
    mine = (kind[None] == 1) & (owner[None] == device)
    place = np.where(mine, lay.value_own + block[None] % blocks, place).astype(np.float32)

    def whole(array):
        return jnp.asarray(np.broadcast_to(array[None], (n, width)))

    before = (np.arange(n, dtype=np.int32) * blocks - 1)[:, None]
    picks = jnp.concatenate([sort_index.reshape(n, blocks), jnp.asarray(before)], axis=1)
    picks = jnp.pad(picks, ((0, 0), (0, LANES - blocks - 1)), constant_values=-1)
    table = pl.pallas_call(
        functools.partial(table_kernel, lay=lay),
        out_shape=jax.ShapeDtypeStruct((lay.rows + 1, n, LANES), jnp.int32),
        in_specs=[VMEM] * 5,
        out_specs=VMEM,
        name="routing_table",
    )(picks, whole(owner), whole(block), whole(kind), jnp.asarray(place))
    mine = lax.dynamic_slice(table, (0, lax.axis_index("ctx"), 0), (lay.rows + 1, 1, ROW))
    return mine.reshape((lay.rows + 1) * ROW)


def routes(ctx_size):
    up = [(d, d + 2) for d in range(ctx_size - 2)]
    down = [(d + 2, d) for d in range(ctx_size - 2)]
    over = [(d, d ^ 1) for d in range(ctx_size)]
    return up, down, over


def copies(jobs, sems):
    started = []
    for k, (valid, source, target) in enumerate(jobs):
        copy = pltpu.make_async_copy(source, target, sems.at[k])
        pl.when(valid)(copy.start)
        started.append((valid, copy))
    for valid, copy in started:
        pl.when(valid)(copy.wait)


def entry(tab_ref, t, k):
    return tab_ref[(t + LEAD) * ROW + k]


def place_of(code):
    return jnp.maximum(code, 0) & (FIRST - 1)


def fill_kernel(tab_ref, key_ref, value_ref, pool_ref, held_ref, sems, *, lay):
    blocks = lay.blocks
    level = tab_ref[lay.device] >> 1
    loads = [
        pltpu.make_async_copy(key_ref, held_ref.at[pl.ds(0, blocks)], sems.at[0]),
        pltpu.make_async_copy(value_ref, held_ref.at[pl.ds(blocks, blocks)], sems.at[1]),
    ]
    stores = [
        pltpu.make_async_copy(
            held_ref.at[pl.ds(0, blocks)], pool_ref.at[pl.ds(level * blocks, blocks)], sems.at[2]
        ),
        pltpu.make_async_copy(
            held_ref.at[pl.ds(blocks, blocks)],
            pool_ref.at[pl.ds(lay.value_own, blocks)],
            sems.at[3],
        ),
    ]
    for load in loads:
        load.start()
    for load, store in zip(loads, stores):
        load.wait()
        store.start()
    for store in stores:
        store.wait()


def first_kernel(tab_ref, key_ref, value_ref, up_ref, down_ref, over_ref, held_ref, sems, *, lay):
    blocks = lay.blocks
    level = tab_ref[lay.device] >> 1
    loads, stores = [], []
    for k, out in enumerate((up_ref, down_ref, over_ref)):
        code = entry(tab_ref, 0, k)
        at = place_of(code)
        is_value = at >= lay.value_own
        key_at = jnp.clip(at - level * blocks, 0, blocks - 1)
        value_at = jnp.clip(at - lay.value_own, 0, blocks - 1)
        valid = code >= 0
        loads.append((valid & jnp.logical_not(is_value), key_ref.at[key_at], held_ref.at[k]))
        loads.append((valid & is_value, value_ref.at[value_at], held_ref.at[k]))
        stores.append((valid, held_ref.at[k], out))
    copies(loads, sems)
    copies(stores, sems)


def store_arrived(t, tab_ref, arrived, pool_ref, held_ref, sems):
    codes = [entry(tab_ref, t, 3 + k) for k in range(3)]
    copies([(c >= 0, got, held_ref.at[k]) for k, (c, got) in enumerate(zip(codes, arrived))], sems)
    copies(
        [(c >= 0, held_ref.at[k], pool_ref.at[place_of(c)]) for k, c in enumerate(codes)], sems
    )


def take_out(codes, outs, pool_ref, held_ref, sems):
    copies(
        [(c >= 0, pool_ref.at[place_of(c)], held_ref.at[k]) for k, c in enumerate(codes)], sems
    )
    copies([(c >= 0, held_ref.at[k], out) for k, (c, out) in enumerate(zip(codes, outs))], sems)


def step_kernel(
    t_ref, tab_ref, pool_in, in_up, in_down, in_over, pool_ref, up_ref, down_ref, over_ref,
    held_ref, sems,
):
    del pool_in
    t = t_ref[0]
    store_arrived(t - 2, tab_ref, (in_up, in_down, in_over), pool_ref, held_ref, sems)
    codes = [entry(tab_ref, t, k) for k in range(3)]
    take_out(codes, (up_ref, down_ref, over_ref), pool_ref, held_ref, sems)


def close_kernel(t_ref, tab_ref, pool_in, *refs):
    del pool_in
    older, newer, (pool_ref, held_ref, sems) = refs[:3], refs[3:6], refs[6:]
    t = t_ref[0]
    store_arrived(t - 2, tab_ref, older, pool_ref, held_ref, sems)
    store_arrived(t - 1, tab_ref, newer, pool_ref, held_ref, sems)


def traffic(byte_count):
    return pl.CostEstimate(flops=0, bytes_accessed=byte_count, transcendentals=0)


def send_all(sends, perms):
    return tuple(lax.ppermute(s, "ctx", p) for s, p in zip(sends, perms))


def slot_number(t):
    return jnp.full((1,), t, jnp.int32) if isinstance(t, int) else t.reshape(1)


def gather_blocks(keys, values, tab, lay):
    one = jax.ShapeDtypeStruct(keys.shape[1:], keys.dtype)
    pool_shape = jax.ShapeDtypeStruct((lay.places,) + one.shape, one.dtype)
    size = 2 * math.prod(one.shape)
    perms = routes(lay.ctx_size)
    three = [pltpu.VMEM((3,) + one.shape, one.dtype), pltpu.SemaphoreType.DMA((3,))]

    sends = pl.pallas_call(
        functools.partial(first_kernel, lay=lay),
        out_shape=(one,) * 3,
        in_specs=[SMEM, ANY, ANY],
        out_specs=(ANY,) * 3,
        scratch_shapes=[three[0], pltpu.SemaphoreType.DMA((6,))],
        compiler_params=BIG,
        cost_estimate=traffic(size * 6),
        name="gather_first",
    )(tab, keys, values)
    older = send_all(sends, perms)
    pool = pl.pallas_call(
        functools.partial(fill_kernel, lay=lay),
        out_shape=pool_shape,
        in_specs=[SMEM, ANY, ANY],
        out_specs=ANY,
        scratch_shapes=[
            pltpu.VMEM((2 * lay.blocks,) + one.shape, one.dtype),
            pltpu.SemaphoreType.DMA((4,)),
        ],
        compiler_params=BIG,
        cost_estimate=traffic(size * 4 * lay.blocks),
        name="gather_fill",
    )(tab, keys, values)

    def step(t, pool, got):
        pool, *sends = pl.pallas_call(
            step_kernel,
            out_shape=(pool_shape, one, one, one),
            in_specs=[SMEM, SMEM] + [ANY] * 4,
            out_specs=(ANY,) * 4,
            scratch_shapes=three,
            input_output_aliases={2: 0},
            compiler_params=BIG,
            cost_estimate=traffic(size * 12),
            name="gather_step",
        )(slot_number(t), tab, pool, *got)
        return pool, send_all(sends, perms)

    pool, newer = step(1, pool, older)
    for t in range(2, STATIC_SLOTS):
        pool, latest = step(t, pool, older)
        older, newer = newer, latest

    def body(state):
        t, pool, older, newer = state
        pool, latest = step(t, pool, older)
        return t + 1, pool, newer, latest

    t, pool, older, newer = lax.while_loop(
        lambda state: state[0] < tab[lay.total],
        body,
        (jnp.int32(STATIC_SLOTS), pool, older, newer),
    )
    return pl.pallas_call(
        close_kernel,
        out_shape=pool_shape,
        in_specs=[SMEM, SMEM] + [ANY] * 7,
        out_specs=ANY,
        scratch_shapes=three,
        input_output_aliases={2: 0},
        compiler_params=BIG,
        cost_estimate=traffic(size * 12),
        name="gather_close",
    )(slot_number(t), tab, pool, *older, *newer)


def add_back(t, tab_ref, arrived, pool_ref, held_ref, got_ref, sems):
    codes = [entry(tab_ref, t, k) for k in range(3)]
    places = [place_of(c) for c in codes]
    valid = [c >= 0 for c in codes]
    fresh = [c >= FIRST for c in codes]
    jobs = [(v, got, got_ref.at[k]) for k, (v, got) in enumerate(zip(valid, arrived))]
    jobs += [
        (v & jnp.logical_not(f), pool_ref.at[p], held_ref.at[k])
        for k, (v, f, p) in enumerate(zip(valid, fresh, places))
    ]
    copies(jobs, sems)
    as_0 = [False, valid[1] & valid[0] & (places[1] == places[0])]
    as_0.append(valid[2] & valid[0] & (places[2] == places[0]))
    as_1 = valid[2] & valid[1] & (places[2] == places[1]) & jnp.logical_not(as_0[2])
    alone = [
        valid[0],
        valid[1] & jnp.logical_not(as_0[1]),
        valid[2] & jnp.logical_not(as_0[2] | as_1),
    ]
    adds = [(0, 0, alone[0]), (1, 1, alone[1]), (1, 0, as_0[1])]
    adds += [(2, 2, alone[2]), (2, 0, as_0[2]), (2, 1, as_1)]
    for k, at, here in adds:
        if k == at:

            @pl.when(here & fresh[k])
            def _(k=k):
                held_ref[k] = got_ref[k]

            here = here & jnp.logical_not(fresh[k])

        @pl.when(here)
        def _(k=k, at=at):
            held_ref[at] = (
                held_ref[at].astype(jnp.float32) + got_ref[k].astype(jnp.float32)
            ).astype(held_ref.dtype)

    copies(
        [(a, held_ref.at[k], pool_ref.at[p]) for k, (a, p) in enumerate(zip(alone, places))], sems
    )


def back_kernel(
    t_ref, tab_ref, pool_in, in_up, in_down, in_over, pool_ref, up_ref, down_ref, over_ref,
    held_ref, got_ref, sems,
):
    del pool_in
    t = t_ref[0]
    add_back(t + 2, tab_ref, (in_up, in_down, in_over), pool_ref, held_ref, got_ref, sems)
    codes = [entry(tab_ref, t, 3 + k) for k in range(3)]
    take_out(codes, (up_ref, down_ref, over_ref), pool_ref, held_ref, sems)


def home_kernel(tab_ref, pool_in, *refs, lay):
    del pool_in
    older, newer, refs = refs[:3], refs[3:6], refs[6:]
    pool_ref, key_ref, value_ref, held_ref, got_ref, own_ref, sems = refs
    blocks = lay.blocks
    level = tab_ref[lay.device] >> 1
    add_back(1, tab_ref, older, pool_ref, held_ref, got_ref, sems)
    add_back(0, tab_ref, newer, pool_ref, held_ref, got_ref, sems)
    halves = (
        (pool_ref.at[pl.ds(level * blocks, blocks)], key_ref),
        (pool_ref.at[pl.ds(lay.value_own, blocks)], value_ref),
    )
    loads, stores = [], []
    for k, (source, target) in enumerate(halves):
        held = own_ref.at[pl.ds(k * blocks, blocks)]
        loads.append(pltpu.make_async_copy(source, held, sems.at[k]))
        stores.append(pltpu.make_async_copy(held, target, sems.at[2 + k]))
    for load in loads:
        load.start()
    for load, store in zip(loads, stores):
        load.wait()
        store.start()
    for store in stores:
        store.wait()


def return_blocks(pool, tab, lay):
    one = jax.ShapeDtypeStruct(pool.shape[1:], pool.dtype)
    pool_shape = jax.ShapeDtypeStruct(pool.shape, pool.dtype)
    own_shape = jax.ShapeDtypeStruct((lay.blocks,) + one.shape, one.dtype)
    size = 2 * math.prod(one.shape)
    up, down, over = routes(lay.ctx_size)
    perms = ([(b, a) for a, b in up], [(b, a) for a, b in down], over)
    buffers = [pltpu.VMEM((3,) + one.shape, one.dtype)] * 2

    def step(t, pool, got):
        pool, *sends = pl.pallas_call(
            back_kernel,
            out_shape=(pool_shape, one, one, one),
            in_specs=[SMEM, SMEM] + [ANY] * 4,
            out_specs=(ANY,) * 4,
            scratch_shapes=buffers + [pltpu.SemaphoreType.DMA((6,))],
            input_output_aliases={2: 0},
            compiler_params=BIG,
            cost_estimate=traffic(size * 15),
            name="return_step",
        )(slot_number(t), tab, pool, *got)
        return pool, send_all(sends, perms)

    def body(state):
        t, pool, older, newer = state
        pool, latest = step(t, pool, older)
        return t - 1, pool, newer, latest

    nothing = (jnp.zeros(one.shape, one.dtype),) * 3
    _, pool, older, newer = lax.while_loop(
        lambda state: state[0] >= STATIC_SLOTS,
        body,
        (tab[lay.total] - 1, pool, nothing, nothing),
    )
    for t in range(STATIC_SLOTS - 1, -1, -1):
        pool, latest = step(t, pool, older)
        older, newer = newer, latest
    return pl.pallas_call(
        functools.partial(home_kernel, lay=lay),
        out_shape=(pool_shape, own_shape, own_shape),
        in_specs=[SMEM] + [ANY] * 7,
        out_specs=(ANY, ANY, ANY),
        scratch_shapes=buffers
        + [
            pltpu.VMEM((2 * lay.blocks,) + one.shape, one.dtype),
            pltpu.SemaphoreType.DMA((6,)),
        ],
        input_output_aliases={1: 0},
        compiler_params=BIG,
        cost_estimate=traffic(size * 40),
        name="return_home",
    )(tab, pool, *older, *newer)[1:]


QK = (((1,), (1,)), ((), ()))
AB = (((1,), (0,)), ((), ()))
TA = (((0,), (0,)), ((), ()))


def dot(a, b, dims):
    return lax.dot_general(a, b, dims, preferred_element_type=jnp.float32)


def rows_of(i):
    return slice(i * BLOCK, (i + 1) * BLOCK)


def parts_of(i, cols, own_ref, pick_refs):
    blocks = len(pick_refs) - 1
    before = pick_refs[blocks][0, :, cols] if i == 0 else own_ref[i - 1, :, cols]
    return own_ref[i, :, cols], before, pick_refs[i][0, :, cols]


def term_places(tab_ref, lay):
    level = tab_ref[lay.device] >> 1
    result = []
    for base, picks in ((level * lay.blocks, lay.key_picks), (lay.value_own, lay.value_picks)):
        places = [base + o for o in range(lay.blocks)]
        places += [tab_ref[picks + j] for j in range(lay.blocks + 1)]
        result.append(places)
    return result


def forward_kernel(tab_ref, *refs, lay, group):
    blocks = lay.blocks
    count = blocks + 2
    q_ref, key_refs, value_refs = refs[0], refs[1 : 1 + count], refs[1 + count : 1 + 2 * count]
    gain_ref, grad_ref, attended_ref, probs_ref, sums_ref, acc_ref = refs[1 + 2 * count :]
    h = pl.program_id(0)
    causal = lax.broadcasted_iota(jnp.int32, (BLOCK, BLOCK), 1) <= lax.broadcasted_iota(
        jnp.int32, (BLOCK, BLOCK), 0
    )
    hide = jnp.where(tab_ref[lay.device] > 0, 0.0, -jnp.inf).astype(jnp.float32)
    lane = lax.broadcasted_iota(jnp.int32, (BLOCK, LANES), 1)

    @pl.when(h == 0)
    def _():
        acc_ref[...] = jnp.zeros_like(acc_ref)

    for i in range(blocks):
        squares = jnp.zeros((BLOCK, 1), jnp.float32)
        center = jnp.zeros((BLOCK, 1), jnp.float32)
        for g in range(group):
            cols = slice(g * HDIM, (g + 1) * HDIM)
            q = q_ref[rows_of(i), cols]
            scores = [dot(q, k, QK) for k in parts_of(i, cols, key_refs[0], key_refs[1:])]
            scores[0] = jnp.where(causal, scores[0], -jnp.inf)
            if i == 0:
                scores[1] = scores[1] + hide
            top = jnp.max(
                jnp.maximum(jnp.maximum(scores[0], scores[1]), scores[2]), axis=1, keepdims=True
            )
            weights = [jnp.exp2((s - top) * SCALE_LOG2) for s in scores]
            scale = 1.0 / jnp.sum(weights[0] + weights[1] + weights[2], axis=1, keepdims=True)
            attended = 0.0
            values = parts_of(i, cols, value_refs[0], value_refs[1:])
            for j, (w, v) in enumerate(zip(weights, values)):
                low = (w * scale).astype(jnp.bfloat16)
                probs_ref[i, g, :, j * BLOCK : (j + 1) * BLOCK] = low
                attended += dot(low, v, AB)
            attended_ref[rows_of(i), cols] = attended
            lifted = gain_ref[:, cols] * grad_ref[rows_of(i), cols].astype(jnp.float32)
            squares += jnp.sum(attended * attended, axis=1, keepdims=True)
            center += jnp.sum(lifted * attended, axis=1, keepdims=True)
        acc_ref[i] += jnp.where(lane == 0, squares, jnp.where(lane == 1, center, 0.0))

    @pl.when(h == pl.num_programs(0) - 1)
    def _():
        for i in range(blocks):
            sums_ref[:, rows_of(i)] = jnp.transpose(acc_ref[i])[:8]


def backward_kernel(
    tab_ref, q_ref, pool_in, gain_ref, grad_ref, attended_ref, probs_ref, sums_ref,
    normed_ref, gq_ref, pool_ref, rms_ref, acc_ref, out_ref, kv_ref, sems, load_sems,
    *, lay, group,
):
    del pool_in
    blocks = lay.blocks
    h = pl.program_id(0)
    steps = pl.num_programs(0)
    width = group * HDIM
    terms = 2 * blocks + 1
    places = term_places(tab_ref, lay)
    buffer = lax.rem(h, 2)

    def columns(at):
        return pl.ds(pl.multiple_of(at * width, width), width)

    def loads(at, buffer):
        return [
            pltpu.make_async_copy(
                pool_ref.at[places[kind][n], :, columns(at)],
                kv_ref.at[buffer, kind, n],
                load_sems.at[buffer, kind * terms + n],
            )
            for kind in range(2)
            for n in range(terms)
        ]

    @pl.when(h == 0)
    def _():
        for load in loads(0, 0):
            load.start()

    for load in loads(h, buffer):
        load.wait()

    @pl.when(h + 1 < steps)
    def _():
        for load in loads(h + 1, 1 - buffer):
            load.start()

    @pl.when(h == 0)
    def _():
        squares = sums_ref[0:1]
        center = sums_ref[1:2]
        inv = lax.rsqrt(squares / WIDTH + 1e-05)
        factor = inv * inv * inv * center / WIDTH
        both = jnp.concatenate([inv, factor, jnp.zeros((6,) + inv.shape[1:], jnp.float32)], axis=0)
        for i in range(blocks):
            wide = jnp.concatenate([both[:, rows_of(i)]] * (LANES // 8), axis=0)
            rms_ref[i] = jnp.transpose(wide)

    for i in range(blocks):
        inv_rms = rms_ref[i, :, 0:1]
        factor = rms_ref[i, :, 1:2]
        for g in range(group):
            cols = slice(g * HDIM, (g + 1) * HDIM)
            q = q_ref[rows_of(i), cols]
            attended = attended_ref[rows_of(i), cols]
            gain = gain_ref[:, cols]
            normed_ref[rows_of(i), cols] = (attended * inv_rms * gain).astype(jnp.bfloat16)
            lifted = gain * grad_ref[rows_of(i), cols].astype(jnp.float32)
            grad = (inv_rms * lifted - attended * factor).astype(jnp.bfloat16)
            row = jnp.sum(grad.astype(jnp.float32) * attended, axis=1, keepdims=True)
            at = (i, 2 * blocks if i == 0 else i - 1, blocks + i)
            keys = [kv_ref[buffer, 0, n, :, cols] for n in at]
            values = [kv_ref[buffer, 1, n, :, cols] for n in at]
            gq = 0.0
            for j in range(3):
                low = probs_ref[i, g, :, j * BLOCK : (j + 1) * BLOCK]
                gv = dot(low, grad, TA)
                gp = dot(grad, values[j], QK)
                gs = (low.astype(jnp.float32) * (gp - row)).astype(jnp.bfloat16)
                gq += dot(gs, keys[j], AB)
                gk = dot(gs, q, TA) * SCALE
                if j == 1 and i > 0:
                    acc_ref[0, at[j], :, cols] += gk
                    acc_ref[1, at[j], :, cols] += gv
                else:
                    acc_ref[0, at[j], :, cols] = gk
                    acc_ref[1, at[j], :, cols] = gv
            gq_ref[rows_of(i), cols] = (gq * SCALE).astype(jnp.bfloat16)

    jobs = []
    for kind in range(2):
        writes = [steps > 0] * blocks
        for at in range(terms - 1, blocks - 1, -1):
            taken = False
            for to in list(range(blocks)) + list(range(at - 1, blocks - 1, -1)):
                here = (places[kind][at] == places[kind][to]) & jnp.logical_not(taken)
                taken = taken | here

                @pl.when(here)
                def _(kind=kind, at=at, to=to):
                    acc_ref[kind, to] += acc_ref[kind, at]

            writes.insert(blocks, jnp.logical_not(taken))
        for at in range(terms):
            jobs.append((kind, at, places[kind][at], writes[at]))

    def store(n, job, slot_h):
        kind, at, place, valid = job
        return valid, pltpu.make_async_copy(
            out_ref.at[kind, at],
            pool_ref.at[place, :, columns(slot_h)],
            sems.at[n],
        )

    for n, job in enumerate(jobs):
        valid, copy = store(n, job, jnp.maximum(h - 1, 0))
        pl.when(valid & (h > 0))(copy.wait)
    out_ref[...] = acc_ref[...].astype(out_ref.dtype)
    for n, job in enumerate(jobs):
        valid, copy = store(n, job, h)
        pl.when(valid)(copy.start)

    @pl.when(h == steps - 1)
    def _():
        for n, job in enumerate(jobs):
            valid, copy = store(n, job, h)
            pl.when(valid)(copy.wait)


def on_device(queries, key_rows, value_rows, norm_gain, sort_index, grad_normed):
    rows, columns = queries.shape
    blocks = rows // BLOCK
    lay = Layout(lax.axis_size("ctx"), blocks)
    heads = columns // HDIM
    group = 2 if heads % 2 == 0 else 1
    width = group * HDIM
    tab = routing_table(sort_index, lay)
    gain = norm_gain.reshape(1, columns)

    shape3 = (blocks, BLOCK, columns)
    pool = gather_blocks(key_rows.reshape(shape3), value_rows.reshape(shape3), tab, lay)

    row_spec = pl.BlockSpec((rows, width), lambda h, tab: (0, h))
    gain_spec = pl.BlockSpec((1, width), lambda h, tab: (0, h))
    probs_spec = pl.BlockSpec((blocks, group, BLOCK, 3 * BLOCK), lambda h, tab: (0, h, 0, 0))
    sums_spec = pl.BlockSpec((8, rows), lambda h, tab: (0, 0))

    def pick_specs(own, picks):
        specs = [pl.BlockSpec((blocks, BLOCK, width), own)]
        for j in range(blocks + 1):
            specs.append(
                pl.BlockSpec((1, BLOCK, width), lambda h, tab, j=j: (tab[picks + j], 0, h))
            )
        return specs

    pool_specs = pick_specs(lambda h, tab: (tab[lay.device] >> 1, 0, h), lay.key_picks)
    pool_specs += pick_specs(lambda h, tab: (lay.value_own // blocks, 0, h), lay.value_picks)
    common = [row_spec] + pool_specs + [gain_spec, row_spec]
    operands = (queries,) + (pool,) * len(pool_specs) + (gain, grad_normed)

    attended, probs, sums = pl.pallas_call(
        functools.partial(forward_kernel, lay=lay, group=group),
        out_shape=(
            jax.ShapeDtypeStruct((rows, columns), jnp.float32),
            jax.ShapeDtypeStruct((blocks, heads, BLOCK, 3 * BLOCK), jnp.bfloat16),
            jax.ShapeDtypeStruct((8, rows), jnp.float32),
        ),
        grid_spec=pltpu.PrefetchScalarGridSpec(
            num_scalar_prefetch=1,
            grid=(heads // group,),
            in_specs=common,
            out_specs=(row_spec, probs_spec, sums_spec),
            scratch_shapes=[pltpu.VMEM((blocks, BLOCK, LANES), jnp.float32)],
        ),
        compiler_params=BIG,
        cost_estimate=pl.CostEstimate(
            flops=4 * rows * 3 * BLOCK * columns,
            bytes_accessed=50_000_000,
            transcendentals=rows * 3 * BLOCK * heads,
        ),
        name="attention_forward",
    )(tab, *operands)

    sums = lax.psum(sums, "head")

    wide = jax.ShapeDtypeStruct((rows, columns), jnp.bfloat16)
    terms = (2, 2 * blocks + 1, BLOCK, width)
    normed, grad_q, pool = pl.pallas_call(
        functools.partial(backward_kernel, lay=lay, group=group),
        out_shape=(wide, wide, jax.ShapeDtypeStruct(pool.shape, pool.dtype)),
        grid_spec=pltpu.PrefetchScalarGridSpec(
            num_scalar_prefetch=1,
            grid=(heads // group,),
            in_specs=[row_spec, ANY, gain_spec, row_spec, row_spec, probs_spec, sums_spec],
            out_specs=(row_spec, row_spec, ANY),
            scratch_shapes=[
                pltpu.VMEM((blocks, BLOCK, LANES), jnp.float32),
                pltpu.VMEM(terms, jnp.float32),
                pltpu.VMEM(terms, jnp.bfloat16),
                pltpu.VMEM((2,) + terms, jnp.bfloat16),
                pltpu.SemaphoreType.DMA((2 * terms[1],)),
                pltpu.SemaphoreType.DMA((2, 2 * terms[1])),
            ],
        ),
        input_output_aliases={2: 2},
        compiler_params=BIG,
        cost_estimate=pl.CostEstimate(
            flops=8 * rows * 3 * BLOCK * columns,
            bytes_accessed=70_000_000,
            transcendentals=0,
        ),
        name="attention_backward",
    )(tab, queries, pool, gain, grad_normed, attended, probs, sums)
    grad_k, grad_v = return_blocks(pool, tab, lay)
    return normed, grad_q, grad_k.reshape(rows, columns), grad_v.reshape(rows, columns)


def solution(mesh):
    in_specs = (
        P("ctx", "head"),
        P("ctx", "head"),
        P("ctx", "head"),
        P("head"),
        P(),
        P("ctx", "head"),
    )
    out_specs = (P("ctx", "head"), P("ctx", "head"), P("ctx", "head"), P("ctx", "head"))
    return jax.shard_map(
        on_device, mesh=mesh, in_specs=in_specs, out_specs=out_specs, check_vma=False
    )
```

time: 1270 us -> 424 us (0.33)
  waiting for transfers between devices: 536 us -> 71 us
  matrix products: 327 us -> 0 us
  Pallas kernels: 0 us -> 166 us
  local copies, waits for them, and re-layouts: 186 us -> 26.4 us
  blocking collectives: 126 us -> 11.6 us
  starting transfers between devices: 34.7 us -> 141 us
  other arithmetic: 42.7 us -> 0.76 us
    all_to_all x7 -> x0, waiting for transfers between devices: 536 us -> none  [the longest x1 110 us: grads_home(): lax.all_to_all(terms[1].reshape(shaped), 'ctx', split_axis=1, concat_axis...]
    dot_general x22 -> x0, matrix products: 276 us -> none  [the longest x4 102 us: block_backward(): jnp.einsum('hqk,qhd->khd', grad_scores, q_split, preferred_element_type=j...]
    pallas_call x0 -> x24, Pallas kernels: none -> 166 us  [the longest x1 50.9 us: on_device(): pl.pallas_call(functools.partial(backward_kernel, lay=lay, group=group),...]
    ppermute x0 -> x54, starting transfers between devices: none -> 141 us  [send_all(): return tuple((lax.ppermute(s, 'ctx', p) for s, p in zip(sends, perms)))]
    all_to_all x1 -> x0, blocking collectives: 120 us -> none  [from_slices(): lax.all_to_all(select(sliced[1]), 'ctx', split_axis=0, concat_axis=2, til...]
    ppermute x0 -> x54, waiting for transfers between devices: none -> 71 us  [send_all(): return tuple((lax.ppermute(s, 'ctx', p) for s, p in zip(sends, perms)))]
    dynamic_update_slice x36 -> x0, local copies, waits for them, and re-layouts: 52.9 us -> none  [the longest x20 29.6 us: on_device(): lax.map(block_backward, (q_blocks, key_sets, value_sets, block_ids, g_blo...]
    sub x8 -> x0, matrix products: 50.9 us -> none  [probabilities(): weights = jnp.exp(scores - highest)]
  transfers between devices with their start and end apart: 7 -> 54, of which waited for: 7 -> 21; matrix products, arithmetic and copies ran while one was open for 4% -> 0% of each run, Pallas kernels for 0% -> 14%
where the time goes in v1:
time: 424 us; the launch traced here: 420 us
  Pallas kernels  166 us (39%)
  starting transfers between devices  141 us (33%)
  waiting for transfers between devices  71 us (17%)
  local copies, waits for them, and re-layouts  26.4 us (6%)
  blocking collectives  11.6 us (3%)
    ppermute x54, starting transfers between devices, send_all(): return tuple((lax.ppermute(s, 'ctx', p) for s, p in zip(sends, perms)))  141 us
    ppermute x54, waiting for transfers between devices, send_all(): return tuple((lax.ppermute(s, 'ctx', p) for s, p in zip(sends, perms)))  71 us
    pallas_call x1, Pallas kernels, on_device(): pl.pallas_call(functools.partial(backward_kernel, lay=lay, group=group),...  50.9 us
    pallas_call x9, Pallas kernels, step(): pl.pallas_call(back_kernel, out_shape=(pool_shape, one, one, one), in_spe...  32.6 us
    pallas_call x8, Pallas kernels, step(): pl.pallas_call(step_kernel, out_shape=(pool_shape, one, one, one), in_spe...  29.1 us
    pallas_call x1, Pallas kernels, on_device(): pl.pallas_call(functools.partial(forward_kernel, lay=lay, group=group), o...  27.7 us
    unnamed x98, local copies, waits for them, and re-layouts  15.3 us
    psum x1, blocking collectives, on_device(): sums = lax.psum(sums, 'head')  11.6 us
  transfers between devices with their start and end apart: 54, of which 21 were waited for; matrix products, arithmetic and copies ran while one was open for 0% of the time, Pallas kernels for 14%

profile of v1, /device:TPU:0, one launch (start us, length us, event | category | flops | bytes accessed | tf_op | source)
XLA Modules:
  0.0 419.9 jit_solution(7292152074870116989)
XLA Ops:
  28.5 6.1 %collective-permute-done.6.in_up = bf16[256,1280]{1,0:T(8,128)(2,1)S(1)} collective-permute-done((bf16[256,1280]{1,0:T(8,128)(2,1)}, bf16[256,1280]{1,0:T(8,128)(2,1)S(1)}, u32[]{:S(2)}, u32[]{:S(2)}) %collective-permute-start.6) | collective-permute-done | bytes 655392 | tf_op jit(solution)/shard_map/ppermute | solution.py:314
  51.4 5.1 %gather_step.10 = (bf16[46,256,1280]{2,1,0:T(8,128)(2,1)}, bf16[256,1280]{1,0:T(8,128)(2,1)}, bf16[256,1280]{1,0:T(8,128)(2,1)}, bf16[256,1280]{1,0:T(8,128)(2,1)}) custom-call(s32[1]{0:T(128)} %constant.55.clone.1.t_ref, s32[1744]{0:T(1024)} %reshape.41.tab_ref, bf16[46,256,1280]{2,1,0:T(8,128)(2,1)} %get-tuple-element.261.pool_in, ...), custom_call_target="tpu_custom_call", output_to_operand_aliasing={{0}: (2, {})} | custom-call | bytes 7864320 | tf_op jit(solution)/shard_map/gather_step/pallas_call | solution.py:354
  67.6 5.1 %gather_step.11 = (bf16[46,256,1280]{2,1,0:T(8,128)(2,1)}, bf16[256,1280]{1,0:T(8,128)(2,1)}, bf16[256,1280]{1,0:T(8,128)(2,1)}, bf16[256,1280]{1,0:T(8,128)(2,1)}) custom-call(s32[1]{0:T(128)} %constant.54.clone.1.t_ref, s32[1744]{0:T(1024)} %reshape.41.tab_ref, bf16[46,256,1280]{2,1,0:T(8,128)(2,1)} %get-tuple-element.262.pool_in, ...), custom_call_target="tpu_custom_call", output_to_operand_aliasing={{0}: (2, {})} | custom-call | bytes 7864320 | tf_op jit(solution)/shard_map/gather_step/pallas_call | solution.py:354
  72.8 5.6 %collective-permute-start.15 = (bf16[256,1280]{1,0:T(8,128)(2,1)}, bf16[256,1280]{1,0:T(8,128)(2,1)S(1)}, u32[]{:S(2)}, u32[]{:S(2)}) collective-permute-start(bf16[256,1280]{1,0:T(8,128)(2,1)} %get-tuple-element.271), channel_id=1, source_target_pairs={{0,8},{4,12},{8,16},{12,20},{16,24},{20,28},{1,9},{5,13},{9,17},{1... | collective-permute-start | bytes 1966088 | tf_op jit(solution)/shard_map/ppermute | solution.py:314
  82.3 5.7 %gather_step.12 = (bf16[46,256,1280]{2,1,0:T(8,128)(2,1)}, bf16[256,1280]{1,0:T(8,128)(2,1)}, bf16[256,1280]{1,0:T(8,128)(2,1)}, bf16[256,1280]{1,0:T(8,128)(2,1)}) custom-call(s32[1]{0:T(128)} %constant.53.clone.1.t_ref, s32[1744]{0:T(1024)} %reshape.41.tab_ref, bf16[46,256,1280]{2,1,0:T(8,128)(2,1)} %get-tuple-element.266.pool_in, ...), custom_call_target="tpu_custom_call", output_to_operand_aliasing={{0}: (2, {})} | custom-call | bytes 7864320 | tf_op jit(solution)/shard_map/gather_step/pallas_call | solution.py:354
  111.9 9.3 %collective-permute-start.24 = (bf16[256,1280]{1,0:T(8,128)(2,1)}, bf16[256,1280]{1,0:T(8,128)(2,1)S(1)}, u32[]{:S(2)}, u32[]{:S(2)}) collective-permute-start(bf16[256,1280]{1,0:T(8,128)(2,1)} %get-tuple-element.283), channel_id=1, source_target_pairs={{0,8},{4,12},{8,16},{12,20},{16,24},{20,28},{1,9},{5,13},{9,17},{1... | collective-permute-start | bytes 1966088 | tf_op jit(solution)/shard_map/ppermute | solution.py:314
  126.1 8.0 %collective-permute-done.24.in_up = bf16[256,1280]{1,0:T(8,128)(2,1)S(1)} collective-permute-done((bf16[256,1280]{1,0:T(8,128)(2,1)}, bf16[256,1280]{1,0:T(8,128)(2,1)S(1)}, u32[]{:S(2)}, u32[]{:S(2)}) %collective-permute-start.24) | collective-permute-done | bytes 655392 | tf_op jit(solution)/shard_map/ppermute | solution.py:314
  142.5 8.3 %collective-permute-start.27 = (bf16[256,1280]{1,0:T(8,128)(2,1)}, bf16[256,1280]{1,0:T(8,128)(2,1)S(1)}, u32[]{:S(2)}, u32[]{:S(2)}) collective-permute-start(bf16[256,1280]{1,0:T(8,128)(2,1)} %get-tuple-element.287), channel_id=1, source_target_pairs={{0,8},{4,12},{8,16},{12,20},{16,24},{20,28},{1,9},{5,13},{9,17},{1... | collective-permute-start | bytes 1966088 | tf_op jit(solution)/shard_map/ppermute | solution.py:314
  158.5 5.2 %collective-permute-done.31 = bf16[256,1280]{1,0:T(8,128)(2,1)S(1)} collective-permute-done((bf16[256,1280]{1,0:T(8,128)(2,1)}, bf16[256,1280]{1,0:T(8,128)(2,1)S(1)}, u32[]{:S(2)}, u32[]{:S(2)}) %collective-permute-start.31) | collective-permute-done | bytes 655392 | tf_op jit(solution)/shard_map/ppermute | solution.py:314
  166.2 7.6 %collective-permute-done.28 = bf16[256,1280]{1,0:T(8,128)(2,1)S(1)} collective-permute-done((bf16[256,1280]{1,0:T(8,128)(2,1)}, bf16[256,1280]{1,0:T(8,128)(2,1)S(1)}, u32[]{:S(2)}, u32[]{:S(2)}) %collective-permute-start.28) | collective-permute-done | bytes 655392 | tf_op jit(solution)/shard_map/ppermute | solution.py:314
  178.5 27.7 %attention_forward.1 = (f32[1024,1280]{1,0:T(8,128)}, bf16[4,10,256,768]{3,2,1,0:T(8,128)(2,1)}, f32[8,1024]{1,0:T(8,128)}) custom-call(s32[1744]{0:T(1024)} %reshape.41.tab_ref, bf16[1024,1280]{1,0:T(8,128)(2,1)} %q_ref.1, ...), custom_call_target="tpu_custom_call" | custom-call | flops 4026531840 | bytes 50000000 | tf_op jit(solution)/shard_map/attention_forward/pallas_call | solution.py:759
  206.2 11.6 %psum.7.sums_ref = f32[8,1024]{1,0:T(8,128)} all-reduce(f32[8,1024]{1,0:T(8,128)} %get-tuple-element.303), channel_id=1, replica_groups=mesh['ctx'=8,'head'=4] {'head'}, use_global_device_ids=true, to_apply=%region_2.3 | all-reduce | flops 8192 | bytes 65536 | tf_op jit(solution)/shard_map/psum | solution.py:782
  217.7 50.9 %attention_backward.1 = (bf16[1024,1280]{1,0:T(8,128)(2,1)}, bf16[1024,1280]{1,0:T(8,128)(2,1)}, bf16[46,256,1280]{2,1,0:T(8,128)(2,1)}) custom-call(s32[1744]{0:T(1024)} %reshape.41.tab_ref, bf16[1024,1280]{1,0:T(8,128)(2,1)} %q_ref.1, ...), custom_call_target="tpu_custom_call", output_to_operand_aliasing={{2}: (2, {})} | custom-call | flops 8053063680 | bytes 70000000 | tf_op jit(solution)/shard_map/attention_backward/pallas_call | solution.py:786
  311.8 7.3 %collective-permute-start.43 = (bf16[256,1280]{1,0:T(8,128)(2,1)}, bf16[256,1280]{1,0:T(8,128)(2,1)S(1)}, u32[]{:S(2)}, u32[]{:S(2)}) collective-permute-start(bf16[256,1280]{1,0:T(8,128)(2,1)} %get-tuple-element.329), channel_id=1, source_target_pairs={{0,8},{4,12},{8,16},{12,20},{16,24},{20,28},{1,9},{5,13},{9,17},{1... | collective-permute-start | bytes 1966088 | tf_op jit(solution)/shard_map/ppermute | solution.py:314
  325.9 9.7 %collective-permute-start.46 = (bf16[256,1280]{1,0:T(8,128)(2,1)}, bf16[256,1280]{1,0:T(8,128)(2,1)S(1)}, u32[]{:S(2)}, u32[]{:S(2)}) collective-permute-start(bf16[256,1280]{1,0:T(8,128)(2,1)} %get-tuple-element.333), channel_id=1, source_target_pairs={{0,8},{4,12},{8,16},{12,20},{16,24},{20,28},{1,9},{5,13},{9,17},{1... | collective-permute-start | bytes 1966088 | tf_op jit(solution)/shard_map/ppermute | solution.py:314
  337.5 5.2 %return_step.18 = (bf16[46,256,1280]{2,1,0:T(8,128)(2,1)}, bf16[256,1280]{1,0:T(8,128)(2,1)}, bf16[256,1280]{1,0:T(8,128)(2,1)}, bf16[256,1280]{1,0:T(8,128)(2,1)}) custom-call(s32[1]{0:T(128)} %constant.54.clone.1.t_ref, s32[1744]{0:T(1024)} %reshape.41.tab_ref, bf16[46,256,1280]{2,1,0:T(8,128)(2,1)} %get-tuple-element.327.pool_in, ...), custom_call_target="tpu_custom_call", output_to_operand_aliasing={{0}: (2, {})} | custom-call | bytes 9830400 | tf_op jit(solution)/shard_map/return_step/pallas_call | solution.py:483
  344.0 7.0 %collective-permute-start.49 = (bf16[256,1280]{1,0:T(8,128)(2,1)}, bf16[256,1280]{1,0:T(8,128)(2,1)S(1)}, u32[]{:S(2)}, u32[]{:S(2)}) collective-permute-start(bf16[256,1280]{1,0:T(8,128)(2,1)} %get-tuple-element.337), channel_id=1, source_target_pairs={{0,8},{4,12},{8,16},{12,20},{16,24},{20,28},{1,9},{5,13},{9,17},{1... | collective-permute-start | bytes 1966088 | tf_op jit(solution)/shard_map/ppermute | solution.py:314
  353.1 6.4 %return_step.19 = (bf16[46,256,1280]{2,1,0:T(8,128)(2,1)}, bf16[256,1280]{1,0:T(8,128)(2,1)}, bf16[256,1280]{1,0:T(8,128)(2,1)}, bf16[256,1280]{1,0:T(8,128)(2,1)}) custom-call(s32[1]{0:T(128)} %constant.55.clone.1.t_ref, s32[1744]{0:T(1024)} %reshape.41.tab_ref, bf16[46,256,1280]{2,1,0:T(8,128)(2,1)} %get-tuple-element.331.pool_in, ...), custom_call_target="tpu_custom_call", output_to_operand_aliasing={{0}: (2, {})} | custom-call | bytes 9830400 | tf_op jit(solution)/shard_map/return_step/pallas_call | solution.py:483
  367.3 5.9 %return_step.20 = (bf16[46,256,1280]{2,1,0:T(8,128)(2,1)}, bf16[256,1280]{1,0:T(8,128)(2,1)}, bf16[256,1280]{1,0:T(8,128)(2,1)}, bf16[256,1280]{1,0:T(8,128)(2,1)}) custom-call(s32[1]{0:T(128)} %constant.56.clone.1.t_ref, s32[1744]{0:T(1024)} %reshape.41.tab_ref, bf16[46,256,1280]{2,1,0:T(8,128)(2,1)} %get-tuple-element.335.pool_in, ...), custom_call_target="tpu_custom_call", output_to_operand_aliasing={{0}: (2, {})} | custom-call | bytes 9830400 | tf_op jit(solution)/shard_map/return_step/pallas_call | solution.py:483
  374.5 6.1 %collective-permute-start.55 = (bf16[256,1280]{1,0:T(8,128)(2,1)}, bf16[256,1280]{1,0:T(8,128)(2,1)S(1)}, u32[]{:S(2)}, u32[]{:S(2)}) collective-permute-start(bf16[256,1280]{1,0:T(8,128)(2,1)} %get-tuple-element.345), channel_id=1, source_target_pairs={{0,8},{4,12},{8,16},{12,20},{16,24},{20,28},{1,9},{5,13},{9,17},{1... | collective-permute-start | bytes 1966088 | tf_op jit(solution)/shard_map/ppermute | solution.py:314
  382.7 6.1 %return_step.21 = (bf16[46,256,1280]{2,1,0:T(8,128)(2,1)}, bf16[256,1280]{1,0:T(8,128)(2,1)}, bf16[256,1280]{1,0:T(8,128)(2,1)}, bf16[256,1280]{1,0:T(8,128)(2,1)}) custom-call(s32[1]{0:T(128)} %constant.57.clone.1.t_ref, s32[1744]{0:T(1024)} %reshape.41.tab_ref, bf16[46,256,1280]{2,1,0:T(8,128)(2,1)} %get-tuple-element.339.pool_in, ...), custom_call_target="tpu_custom_call", output_to_operand_aliasing={{0}: (2, {})} | custom-call | bytes 9830400 | tf_op jit(solution)/shard_map/return_step/pallas_call | solution.py:483
  390.1 6.8 %collective-permute-start.58 = (bf16[256,1280]{1,0:T(8,128)(2,1)}, bf16[256,1280]{1,0:T(8,128)(2,1)S(1)}, u32[]{:S(2)}, u32[]{:S(2)}) collective-permute-start(bf16[256,1280]{1,0:T(8,128)(2,1)} %get-tuple-element.348), channel_id=1, source_target_pairs={{0,8},{4,12},{8,16},{12,20},{16,24},{20,28},{1,9},{5,13},{9,17},{1... | collective-permute-start | bytes 1966088 | tf_op jit(solution)/shard_map/ppermute | solution.py:314
  397.0 6.7 %collective-permute-done.57.refs_3_ = bf16[256,1280]{1,0:T(8,128)(2,1)S(1)} collective-permute-done((bf16[256,1280]{1,0:T(8,128)(2,1)}, bf16[256,1280]{1,0:T(8,128)(2,1)S(1)}, u32[]{:S(2)}, u32[]{:S(2)}) %collective-permute-start.57) | collective-permute-done | bytes 655392 | tf_op jit(solution)/shard_map/ppermute | solution.py:314
  408.6 11.1 %return_home.1 = (bf16[46,256,1280]{2,1,0:T(8,128)(2,1)}, bf16[4,256,1280]{2,1,0:T(8,128)(2,1)}, bf16[4,256,1280]{2,1,0:T(8,128)(2,1)}) custom-call(s32[1744]{0:T(1024)} %reshape.41.tab_ref, bf16[46,256,1280]{2,1,0:T(8,128)(2,1)} %get-tuple-element.343.pool_in, bf16[256,1280]{1,0:T(8,128)(2,1)} %copy-done.3, ...), custom_call_target="tpu_custom_call", output_to_operand_aliasing={{0}: (1, {})} | custom-call | bytes 26214400 | tf_op jit(solution)/shard_map/return_home/pallas_call | solution.py:510
  (226 shorter events, 184.5 us)
Async XLA Ops:
  56.5 24.4 %collective-permute-start.12 = (bf16[256,1280]{1,0:T(8,128)(2,1)}, bf16[256,1280]{1,0:T(8,128)(2,1)S(1)}, u32[]{:S(2)}, u32[]{:S(2)}) collective-permute-start(bf16[256,1280]{1,0:T(8,128)(2,1)} %get-tuple-element.267), channel_id=1, source_target_pairs={{0,8},{4,12},{8,16},{12,20},{16,24},{20,28},{1,9},{5,13},{9,17},{1... | collective-permute-start | bytes 1966088 | tf_op jit(solution)/shard_map/ppermute | solution.py:314
  60.9 20.3 %collective-permute-start.13 = (bf16[256,1280]{1,0:T(8,128)(2,1)}, bf16[256,1280]{1,0:T(8,128)(2,1)S(1)}, u32[]{:S(2)}, u32[]{:S(2)}) collective-permute-start(bf16[256,1280]{1,0:T(8,128)(2,1)} %get-tuple-element.268), channel_id=1, source_target_pairs={{8,0},{12,4},{16,8},{20,12},{24,16},{28,20},{9,1},{13,5},{17,9},{2... | collective-permute-start | bytes 1966088 | tf_op jit(solution)/shard_map/ppermute | solution.py:314
  72.8 22.1 %collective-permute-start.15 = (bf16[256,1280]{1,0:T(8,128)(2,1)}, bf16[256,1280]{1,0:T(8,128)(2,1)S(1)}, u32[]{:S(2)}, u32[]{:S(2)}) collective-permute-start(bf16[256,1280]{1,0:T(8,128)(2,1)} %get-tuple-element.271), channel_id=1, source_target_pairs={{0,8},{4,12},{8,16},{12,20},{16,24},{20,28},{1,9},{5,13},{9,17},{1... | collective-permute-start | bytes 1966088 | tf_op jit(solution)/shard_map/ppermute | solution.py:314
  88.0 21.0 %collective-permute-start.18 = (bf16[256,1280]{1,0:T(8,128)(2,1)}, bf16[256,1280]{1,0:T(8,128)(2,1)S(1)}, u32[]{:S(2)}, u32[]{:S(2)}) collective-permute-start(bf16[256,1280]{1,0:T(8,128)(2,1)} %get-tuple-element.275), channel_id=1, source_target_pairs={{0,8},{4,12},{8,16},{12,20},{16,24},{20,28},{1,9},{5,13},{9,17},{1... | collective-permute-start | bytes 1966088 | tf_op jit(solution)/shard_map/ppermute | solution.py:314
  101.8 21.2 %collective-permute-start.21 = (bf16[256,1280]{1,0:T(8,128)(2,1)}, bf16[256,1280]{1,0:T(8,128)(2,1)S(1)}, u32[]{:S(2)}, u32[]{:S(2)}) collective-permute-start(bf16[256,1280]{1,0:T(8,128)(2,1)} %get-tuple-element.279), channel_id=1, source_target_pairs={{0,8},{4,12},{8,16},{12,20},{16,24},{20,28},{1,9},{5,13},{9,17},{1... | collective-permute-start | bytes 1966088 | tf_op jit(solution)/shard_map/ppermute | solution.py:314
  111.9 22.2 %collective-permute-start.24 = (bf16[256,1280]{1,0:T(8,128)(2,1)}, bf16[256,1280]{1,0:T(8,128)(2,1)S(1)}, u32[]{:S(2)}, u32[]{:S(2)}) collective-permute-start(bf16[256,1280]{1,0:T(8,128)(2,1)} %get-tuple-element.283), channel_id=1, source_target_pairs={{0,8},{4,12},{8,16},{12,20},{16,24},{20,28},{1,9},{5,13},{9,17},{1... | collective-permute-start | bytes 1966088 | tf_op jit(solution)/shard_map/ppermute | solution.py:314
  140.5 23.1 %collective-permute-start.31 = (bf16[256,1280]{1,0:T(8,128)(2,1)}, bf16[256,1280]{1,0:T(8,128)(2,1)S(1)}, u32[]{:S(2)}, u32[]{:S(2)}) collective-permute-start(bf16[256,1280]{1,0:T(8,128)(2,1)} %get-tuple-element.291), channel_id=1, source_target_pairs={{8,0},{12,4},{16,8},{20,12},{24,16},{28,20},{9,1},{13,5},{17,9},{2... | collective-permute-start | bytes 1966088 | tf_op jit(solution)/shard_map/ppermute | solution.py:314
  141.8 21.8 %collective-permute-start.32 = (bf16[256,1280]{1,0:T(8,128)(2,1)}, bf16[256,1280]{1,0:T(8,128)(2,1)S(1)}, u32[]{:S(2)}, u32[]{:S(2)}) collective-permute-start(bf16[256,1280]{1,0:T(8,128)(2,1)} %get-tuple-element.292), channel_id=1, source_target_pairs={{0,4},{4,0},{8,12},{12,8},{16,20},{20,16},{24,28},{28,24},{1,5},{5... | collective-permute-start | bytes 1966088 | tf_op jit(solution)/shard_map/ppermute | solution.py:314
  142.5 23.7 %collective-permute-start.27 = (bf16[256,1280]{1,0:T(8,128)(2,1)}, bf16[256,1280]{1,0:T(8,128)(2,1)S(1)}, u32[]{:S(2)}, u32[]{:S(2)}) collective-permute-start(bf16[256,1280]{1,0:T(8,128)(2,1)} %get-tuple-element.287), channel_id=1, source_target_pairs={{0,8},{4,12},{8,16},{12,20},{16,24},{20,28},{1,9},{5,13},{9,17},{1... | collective-permute-start | bytes 1966088 | tf_op jit(solution)/shard_map/ppermute | solution.py:314
  150.7 23.0 %collective-permute-start.28 = (bf16[256,1280]{1,0:T(8,128)(2,1)}, bf16[256,1280]{1,0:T(8,128)(2,1)S(1)}, u32[]{:S(2)}, u32[]{:S(2)}) collective-permute-start(bf16[256,1280]{1,0:T(8,128)(2,1)} %get-tuple-element.288), channel_id=1, source_target_pairs={{8,0},{12,4},{16,8},{20,12},{24,16},{28,20},{9,1},{13,5},{17,9},{2... | collective-permute-start | bytes 1966088 | tf_op jit(solution)/shard_map/ppermute | solution.py:314
  279.9 24.9 %collective-permute-start.36 = (bf16[256,1280]{1,0:T(8,128)(2,1)}, bf16[256,1280]{1,0:T(8,128)(2,1)S(1)}, u32[]{:S(2)}, u32[]{:S(2)}) collective-permute-start(bf16[256,1280]{1,0:T(8,128)(2,1)} %get-tuple-element.320), channel_id=1, source_target_pairs={{8,0},{12,4},{16,8},{20,12},{24,16},{28,20},{9,1},{13,5},{17,9},{2... | collective-permute-start | bytes 1966088 | tf_op jit(solution)/shard_map/ppermute | solution.py:314
  281.2 25.2 %collective-permute-start.37 = (bf16[256,1280]{1,0:T(8,128)(2,1)}, bf16[256,1280]{1,0:T(8,128)(2,1)S(1)}, u32[]{:S(2)}, u32[]{:S(2)}) collective-permute-start(bf16[256,1280]{1,0:T(8,128)(2,1)} %get-tuple-element.321), channel_id=1, source_target_pairs={{0,8},{4,12},{8,16},{12,20},{16,24},{20,28},{1,9},{5,13},{9,17},{1... | collective-permute-start | bytes 1966088 | tf_op jit(solution)/shard_map/ppermute | solution.py:314
  298.8 20.3 %collective-permute-start.39 = (bf16[256,1280]{1,0:T(8,128)(2,1)}, bf16[256,1280]{1,0:T(8,128)(2,1)S(1)}, u32[]{:S(2)}, u32[]{:S(2)}) collective-permute-start(bf16[256,1280]{1,0:T(8,128)(2,1)} %get-tuple-element.324), channel_id=1, source_target_pairs={{8,0},{12,4},{16,8},{20,12},{24,16},{28,20},{9,1},{13,5},{17,9},{2... | collective-permute-start | bytes 1966088 | tf_op jit(solution)/shard_map/ppermute | solution.py:314
  300.1 21.0 %collective-permute-start.40 = (bf16[256,1280]{1,0:T(8,128)(2,1)}, bf16[256,1280]{1,0:T(8,128)(2,1)S(1)}, u32[]{:S(2)}, u32[]{:S(2)}) collective-permute-start(bf16[256,1280]{1,0:T(8,128)(2,1)} %get-tuple-element.325), channel_id=1, source_target_pairs={{0,8},{4,12},{8,16},{12,20},{16,24},{20,28},{1,9},{5,13},{9,17},{1... | collective-permute-start | bytes 1966088 | tf_op jit(solution)/shard_map/ppermute | solution.py:314
  310.5 25.1 %collective-permute-start.42 = (bf16[256,1280]{1,0:T(8,128)(2,1)}, bf16[256,1280]{1,0:T(8,128)(2,1)S(1)}, u32[]{:S(2)}, u32[]{:S(2)}) collective-permute-start(bf16[256,1280]{1,0:T(8,128)(2,1)} %get-tuple-element.328), channel_id=1, source_target_pairs={{8,0},{12,4},{16,8},{20,12},{24,16},{28,20},{9,1},{13,5},{17,9},{2... | collective-permute-start | bytes 1966088 | tf_op jit(solution)/shard_map/ppermute | solution.py:314
  311.8 24.6 %collective-permute-start.43 = (bf16[256,1280]{1,0:T(8,128)(2,1)}, bf16[256,1280]{1,0:T(8,128)(2,1)S(1)}, u32[]{:S(2)}, u32[]{:S(2)}) collective-permute-start(bf16[256,1280]{1,0:T(8,128)(2,1)} %get-tuple-element.329), channel_id=1, source_target_pairs={{0,8},{4,12},{8,16},{12,20},{16,24},{20,28},{1,9},{5,13},{9,17},{1... | collective-permute-start | bytes 1966088 | tf_op jit(solution)/shard_map/ppermute | solution.py:314
  324.6 26.4 %collective-permute-start.45 = (bf16[256,1280]{1,0:T(8,128)(2,1)}, bf16[256,1280]{1,0:T(8,128)(2,1)S(1)}, u32[]{:S(2)}, u32[]{:S(2)}) collective-permute-start(bf16[256,1280]{1,0:T(8,128)(2,1)} %get-tuple-element.332), channel_id=1, source_target_pairs={{8,0},{12,4},{16,8},{20,12},{24,16},{28,20},{9,1},{13,5},{17,9},{2... | collective-permute-start | bytes 1966088 | tf_op jit(solution)/shard_map/ppermute | solution.py:314
  325.9 26.2 %collective-permute-start.46 = (bf16[256,1280]{1,0:T(8,128)(2,1)}, bf16[256,1280]{1,0:T(8,128)(2,1)S(1)}, u32[]{:S(2)}, u32[]{:S(2)}) collective-permute-start(bf16[256,1280]{1,0:T(8,128)(2,1)} %get-tuple-element.333), channel_id=1, source_target_pairs={{0,8},{4,12},{8,16},{12,20},{16,24},{20,28},{1,9},{5,13},{9,17},{1... | collective-permute-start | bytes 1966088 | tf_op jit(solution)/shard_map/ppermute | solution.py:314
  342.7 22.7 %collective-permute-start.48 = (bf16[256,1280]{1,0:T(8,128)(2,1)}, bf16[256,1280]{1,0:T(8,128)(2,1)S(1)}, u32[]{:S(2)}, u32[]{:S(2)}) collective-permute-start(bf16[256,1280]{1,0:T(8,128)(2,1)} %get-tuple-element.336), channel_id=1, source_target_pairs={{8,0},{12,4},{16,8},{20,12},{24,16},{28,20},{9,1},{13,5},{17,9},{2... | collective-permute-start | bytes 1966088 | tf_op jit(solution)/shard_map/ppermute | solution.py:314
  344.0 22.3 %collective-permute-start.49 = (bf16[256,1280]{1,0:T(8,128)(2,1)}, bf16[256,1280]{1,0:T(8,128)(2,1)S(1)}, u32[]{:S(2)}, u32[]{:S(2)}) collective-permute-start(bf16[256,1280]{1,0:T(8,128)(2,1)} %get-tuple-element.337), channel_id=1, source_target_pairs={{0,8},{4,12},{8,16},{12,20},{16,24},{20,28},{1,9},{5,13},{9,17},{1... | collective-permute-start | bytes 1966088 | tf_op jit(solution)/shard_map/ppermute | solution.py:314
  359.5 21.1 %collective-permute-start.51 = (bf16[256,1280]{1,0:T(8,128)(2,1)}, bf16[256,1280]{1,0:T(8,128)(2,1)S(1)}, u32[]{:S(2)}, u32[]{:S(2)}) collective-permute-start(bf16[256,1280]{1,0:T(8,128)(2,1)} %get-tuple-element.340), channel_id=1, source_target_pairs={{8,0},{12,4},{16,8},{20,12},{24,16},{28,20},{9,1},{13,5},{17,9},{2... | collective-permute-start | bytes 1966088 | tf_op jit(solution)/shard_map/ppermute | solution.py:314
  360.8 20.9 %collective-permute-start.52 = (bf16[256,1280]{1,0:T(8,128)(2,1)}, bf16[256,1280]{1,0:T(8,128)(2,1)S(1)}, u32[]{:S(2)}, u32[]{:S(2)}) collective-permute-start(bf16[256,1280]{1,0:T(8,128)(2,1)} %get-tuple-element.341), channel_id=1, source_target_pairs={{0,8},{4,12},{8,16},{12,20},{16,24},{20,28},{1,9},{5,13},{9,17},{1... | collective-permute-start | bytes 1966088 | tf_op jit(solution)/shard_map/ppermute | solution.py:314
  373.2 23.7 %collective-permute-start.54 = (bf16[256,1280]{1,0:T(8,128)(2,1)}, bf16[256,1280]{1,0:T(8,128)(2,1)S(1)}, u32[]{:S(2)}, u32[]{:S(2)}) collective-permute-start(bf16[256,1280]{1,0:T(8,128)(2,1)} %get-tuple-element.344), channel_id=1, source_target_pairs={{8,0},{12,4},{16,8},{20,12},{24,16},{28,20},{9,1},{13,5},{17,9},{2... | collective-permute-start | bytes 1966088 | tf_op jit(solution)/shard_map/ppermute | solution.py:314
  374.5 22.5 %collective-permute-start.55 = (bf16[256,1280]{1,0:T(8,128)(2,1)}, bf16[256,1280]{1,0:T(8,128)(2,1)S(1)}, u32[]{:S(2)}, u32[]{:S(2)}) collective-permute-start(bf16[256,1280]{1,0:T(8,128)(2,1)} %get-tuple-element.345), channel_id=1, source_target_pairs={{0,8},{4,12},{8,16},{12,20},{16,24},{20,28},{1,9},{5,13},{9,17},{1... | collective-permute-start | bytes 1966088 | tf_op jit(solution)/shard_map/ppermute | solution.py:314
  (79 other events, 637.1 us)
